TPU v7x, 32 devices: a whole 2x2x4 slice. The times are simulated.
32 devices in a mesh: batch: 4 (over z), pos: 8 (over y, x, core).
Axes of the slice: x: 2, y: 2, z: 4, core: 2. Of those that a mesh axis runs over, the one named last changes fastest.
Arguments:
- inputs: bfloat16 [4, 4096, 1536], P('batch', 'pos'), may hold values from -6 to 6
- bn_scale: float32 [1536], replicated, may hold values from 0.25 to 1.75
- bn_shift: float32 [1536], replicated, may hold values from -2 to 2
- mid_scale: float32 [384], replicated, may hold values from 0.25 to 1.75
- mid_shift: float32 [384], replicated, may hold values from -2 to 2
- dilated_weight: bfloat16 [1536, 3, 384], P('batch'), may hold values from -0.09375 to 0.09375
- w_point: bfloat16 [384, 1536], P('batch'), may hold values from -0.3125 to 0.3125
- head: bfloat16 [5120, 1536], P('pos'), may hold values from -0.15625 to 0.15625
- targets: bfloat16 [4, 4096, 512], P('batch', 'pos'), may hold values from 0 to 2
- assay_slots: int32 [4, 512], P('batch', 'pos'), may hold values from 0 to 639, as said below
- assay_counts: int32 [4, 8], P('batch', 'pos'), may hold values from 1 to 64, as said below
Outputs:
- d_inputs: bfloat16 [4, 4096, 1536], P('batch', 'pos')
- new_head: bfloat16 [5120, 1536], P('pos')
Inputs may be any that keep to these rules, and one draw needn't show every extreme that they name: `assay_slots`: within each block of 64 slots (one shard of one sequence) the entries are distinct. `assay_counts`: in every sequence some shard has all 64 slots live.
All inputs are finite; a program needn't handle non-finite values.
Results may differ from a plain program's by a relative error of at most 0.012.
Values may be sent and summed in bfloat16 or wider, within the bound.
A program may use at most 64 MiB of HBM per device.

v0:
```python
import jax
import jax.numpy as jnp
from jax import lax
from jax.sharding import PartitionSpec as P

DILATION_STEP = 32


def with_halo(shard, sides, width):
    for axis, dim in sides:
        peers, length = (lax.axis_size(axis), shard.shape[dim])
        up = [(i, (i + 1) % peers) for i in range(peers - 1)]
        down = [(j, i) for i, j in up]
        last = lax.slice_in_dim(shard, length - width, length, axis=dim)
        initial = lax.slice_in_dim(shard, 0, width, axis=dim)
        before = lax.ppermute(last, axis, up)
        after = lax.ppermute(initial, axis, down)
        shard = jnp.concatenate([before, shard, after], axis=dim)
    return shard


def gelu_slope(value):
    return jax.jvp(jax.nn.gelu, (value,), (jnp.ones_like(value),))[1]


def per_device(
    inputs,
    bn_scale,
    bn_shift,
    mid_scale,
    mid_shift,
    dilated_weight,
    w_point,
    head,
    targets,
    assay_slots,
    assay_counts,
):
    contract = (((1,), (1,)), ((), ()))
    kernel, pointwise = (
        lax.all_gather(dilated_weight, "batch", axis=0, tiled=True),
        lax.all_gather(w_point, "batch", axis=0, tiled=True),
    )
    stream = inputs[0]
    rows = stream.shape[0]
    window_length = DILATION_STEP
    first = stream.astype(jnp.float32) * bn_scale + bn_shift
    acted = jax.nn.gelu(first).astype(jnp.bfloat16)
    padded_input = with_halo(acted, (("pos", 0),), window_length)
    hidden_state = jnp.dot(
        padded_input[0:rows], kernel[:, 0, :], preferred_element_type=jnp.float32
    )
    hidden_state = hidden_state + jnp.dot(
        padded_input[window_length : window_length + rows],
        kernel[:, 1, :],
        preferred_element_type=jnp.float32,
    )
    hidden_state = hidden_state + jnp.dot(
        padded_input[2 * window_length : 2 * window_length + rows],
        kernel[:, 2, :],
        preferred_element_type=jnp.float32,
    )
    second = hidden_state * mid_scale + mid_shift
    mid = jax.nn.gelu(second).astype(jnp.bfloat16)
    embed = (
        stream.astype(jnp.float32) + jnp.dot(mid, pointwise, preferred_element_type=jnp.float32)
    ).astype(jnp.bfloat16)
    slots = assay_slots[0]
    slot_count = slots.shape[0]
    chosen = head[slots]
    live_mark = (jnp.arange(slot_count) < assay_counts[0, 0]).astype(jnp.bfloat16)
    selected, live_all = (
        lax.all_gather(chosen, "pos", axis=0, tiled=True),
        lax.all_gather(live_mark, "pos", axis=0, tiled=True),
    )
    pre = lax.dot_general(embed, selected, contract, preferred_element_type=jnp.float32)
    goal = targets[0].astype(jnp.float32)
    delta = (
        live_all.astype(jnp.float32) * (jax.nn.softplus(pre) - goal) * jax.nn.sigmoid(pre)
    ).astype(jnp.bfloat16)
    back = jnp.dot(delta, selected, preferred_element_type=jnp.float32).astype(jnp.bfloat16)
    dmid = lax.dot_general(back, pointwise, contract, preferred_element_type=jnp.float32)
    dhid = (dmid * gelu_slope(second) * mid_scale).astype(jnp.bfloat16)
    padded_grad = with_halo(dhid, (("pos", 0),), window_length)
    dact = lax.dot_general(
        padded_grad[2 * window_length : 2 * window_length + rows],
        kernel[:, 0, :],
        contract,
        preferred_element_type=jnp.float32,
    )
    dact = dact + lax.dot_general(
        padded_grad[window_length : window_length + rows],
        kernel[:, 1, :],
        contract,
        preferred_element_type=jnp.float32,
    )
    dact = dact + lax.dot_general(
        padded_grad[0:rows], kernel[:, 2, :], contract, preferred_element_type=jnp.float32
    )
    d_inputs = (back.astype(jnp.float32) + dact * gelu_slope(first) * bn_scale).astype(jnp.bfloat16)
    owned = lax.psum_scatter(
        lax.dot_general(
            delta, embed, (((0,), (0,)), ((), ())), preferred_element_type=jnp.float32
        ).astype(jnp.bfloat16),
        "pos",
        scatter_dimension=0,
        tiled=True,
    ).astype(jnp.float32)
    spread = jnp.zeros((head.shape[0], owned.shape[1]), jnp.float32).at[slots].add(owned)
    d_head = lax.psum(spread.astype(jnp.bfloat16), "batch").astype(jnp.float32)
    new_head = (head.astype(jnp.float32) - 0.004 * d_head).astype(jnp.bfloat16)
    return (d_inputs[None], new_head)


def solution(mesh):
    in_specs = (
        P("batch", "pos", None),
        P(),
        P(),
        P(),
        P(),
        P("batch", None, None),
        P("batch", None),
        P("pos", None),
        P("batch", "pos", None),
        P("batch", "pos"),
        P("batch", "pos"),
    )
    out_specs = (P("batch", "pos", None), P("pos", None))
    return jax.shard_map(
        per_device, mesh=mesh, in_specs=in_specs, out_specs=out_specs, check_vma=False
    )
```

profile of v0, /device:TPU:0, one launch (start us, length us, event | category | flops | bytes accessed | tf_op | source)
XLA Modules:
  0.0 286.1 jit_solution(2264082619135657359)
XLA Ops:
  7.2 0.0 copy-start.11
  7.2 0.0 copy-start.1
  7.2 0.0 copy-start.4
  7.2 0.0 copy-start.5
  7.2 0.0 all-gather.5.cloned.1.call-start
  7.3 0.7 all-gather.5.cloned.1.call-update
  7.9 0.0 all-gather.7.cloned.1.call-start
  8.0 0.7 all-gather.7.cloned.1.call-update
  8.7 0.0 all-gather.9.cloned.1.call-start
  8.7 0.7 fusion.71
  9.4 3.4 %gather_fusion = bf16[64,1536]{1,0:T(8,128)(2,1)} fusion(bf16[640,1536]{1,0:T(8,128)(2,1)} %param.18, s32[1024]{0:T(1024)S(1)} %pad_clamp_fusion), kind=kCustom, calls=%fused_computation | custom fusion | bytes 393472 | tf_op jit(solution)/shard_map/gather | solution.py:70
  12.8 0.0 all-gather.9.cloned.1.call-update
  12.8 0.0 reduce-scatter.2.cloned.1.call-start
  12.9 0.0 copy-done.1
  12.9 0.0 copy-done.4
  12.9 0.0 copy-done.5
  12.9 1.3 fusion.12
  14.2 2.4 collective-permute-start
  16.6 1.3 collective-permute-start.1
  18.5 0.0 copy-done.11
  18.5 0.6 dynamic-slice
  19.7 0.2 dynamic-update-slice
  19.9 17.5 %all-reduce = bf16[512]{0:T(512)(128)(2,1)S(1)} all-reduce(bf16[512]{0:T(512)(128)(2,1)S(1)} %dynamic-update-slice), channel_id=1, replica_groups=mesh['batch'=4,'pos'=8] {'pos'}, use_global_device_ids=true, to_apply=%add | all-reduce | flops 512 | bytes 2048
  37.4 44.9 %all-gather.5.cloned.1.call-done = bf16[1536,3,384]{2,0,1:T(8,128)(2,1)} async-done(((bf16[384,3,384]{2,0,1:T(8,128)(2,1)}), bf16[1536,3,384]{2,0,1:T(8,128)(2,1)}) %all-gather.5.cloned.1.call-update) | async-done | bytes 3538960 | tf_op jit(solution)/shard_map/all_gather | solution.py:41
  82.3 2.8 fusion.38
  85.2 0.0 copy-start.10
  85.2 0.0 collective-permute-done.1
  85.2 0.0 copy-done.2
  85.2 1.9 fusion.34
  87.1 0.0 collective-permute-done
  87.1 0.0 copy-done.9
  87.1 0.0 copy-done.10
  87.1 1.9 fusion.44
  89.0 23.9 %all-gather.7.cloned.1.call-done = bf16[384,1536]{1,0:T(8,128)(2,1)} async-done(((bf16[96,1536]{1,0:T(8,128)(2,1)}), bf16[384,1536]{1,0:T(8,128)(2,1)}) %all-gather.7.cloned.1.call-update) | async-done | bytes 1179664 | tf_op jit(solution)/shard_map/all_gather | solution.py:42
  113.0 2.5 fusion.29
  115.5 0.0 copy-start.12
  115.5 24.8 %all-gather.9.cloned.1.call-done = bf16[512,1536]{1,0:T(8,128)(2,1)} async-done(((bf16[64,1536]{1,0:T(8,128)(2,1)}), bf16[512,1536]{1,0:T(8,128)(2,1)}) %all-gather.9.cloned.1.call-update) | async-done | bytes 1572880 | tf_op jit(solution)/shard_map/all_gather | solution.py:73
  140.3 0.0 copy-done.12
  140.3 2.5 fusion.90
  142.8 1.0 copy-done.13
  143.7 4.3 %convolution_convert_fusion = bf16[512,1536]{1,0:T(8,128)(2,1)} fusion(bf16[512,1536]{1,0:T(8,128)(2,1)} %copy-done.12, f32[512,512]{1,0:T(8,128)S(1)} %fusion.90, bf16[1,512,512]{2,1,0:T(8,128)(2,1)S(1)} %copy-done.8, f32[512]{0:T(512)S(1)} %convert_element_type.70), kind=kOutput, calls=%fused_computation.39 | convolution fusion | flops 809762816 | bytes 4720640 | tf_op jit(solution)/shard_map/dot_general | solution.py:102
  148.1 0.0 reduce-scatter.2.cloned.1.call-update
  148.1 0.0 all-reduce.3.cloned.1.call-start
  148.2 4.1 %convolution_convert_fusion.1 = bf16[512,1536]{1,0:T(8,128)(2,1)} fusion(bf16[512,1536]{1,0:T(8,128)(2,1)S(1)} %copy-done.6, f32[512,512]{1,0:T(8,128)} %copy-done.13, bf16[1,512,512]{2,1,0:T(8,128)(2,1)} %param.19, f32[512]{0:T(512)S(1)} %convert_element_type.70), kind=kOutput, calls=%fused_computation.40 | convolution fusion | flops 809762816 | bytes 4720640 | tf_op jit(solution)/shard_map/dot_general | solution.py:81
  152.2 34.5 %reduce-scatter.2.cloned.1.call-done = bf16[64,1536]{1,0:T(8,128)(2,1)} async-done(((bf16[512,1536]{1,0:T(8,128)(2,1)}), bf16[64,1536]{1,0:T(8,128)(2,1)}) %reduce-scatter.2.cloned.1.call-update) | async-done | bytes 196624 | tf_op jit(solution)/shard_map/reduce_scatter | solution.py:101
  186.7 3.7 %scatter_custom_fusion = f32[640,1536]{1,0:T(8,128)} fusion(s32[64]{0:T(128)S(1)} %fusion.71, f32[]{:T(128)} %constant.15.clone.1, bf16[64,1536]{1,0:T(8,128)(2,1)} %reduce-scatter.2.cloned.1.call-done), kind=kCustom, calls=%fused_computation.43 | custom fusion | flops 196608 | bytes 4128772 | tf_op jit(solution)/shard_map/scatter-add | solution.py:109
  190.4 3.7 %convert_element_type.89 = bf16[640,1536]{1,0:T(8,128)(2,1)} convert(f32[640,1536]{1,0:T(8,128)} %scatter_custom_fusion) | non-fusion elementwise | flops 983040 | bytes 5898240 | tf_op jit(solution)/shard_map/convert_element_type | solution.py:110
  194.1 0.0 all-reduce.3.cloned.1.call-update
  194.1 0.0 copy-done.7
  194.1 0.0 copy-start.3
  194.1 3.0 %fusion.45 = bf16[512,384]{1,0:T(8,128)(2,1)S(1)} fusion(bf16[512,1536]{1,0:T(8,128)(2,1)} %convolution_convert_fusion.1, bf16[384,1536]{1,0:T(8,128)(2,1)S(1)} %copy-done.7, f32[512,384]{1,0:T(8,128)} %fusion.44, f32[384]{0:T(512)S(1)} %copy-done.10), kind=kOutput, calls=%fused_computation.59 | convolution fusion | flops 607715328 | bytes 3933696 | tf_op jit(solution)/shard_map/dot_general | solution.py:82
  197.2 1.3 collective-permute-start.2
  198.5 3.0 %collective-permute-start.3 = (bf16[32,384]{1,0:T(8,128)(2,1)S(1)}, bf16[32,384]{1,0:T(8,128)(2,1)S(1)}, u32[]{:S(2)}, u32[]{:S(2)}) collective-permute-start(bf16[32,384]{1,0:T(8,128)(2,1)S(1)} %get-tuple-element.5), channel_id=1, source_target_pairs={{0,1},{1,2},{2,3},{3,4},{4,5},{5,6},{6,7},{8,9},{9,10},{10,11},{11... | collective-permute-start | bytes 73736 | tf_op jit(solution)/shard_map/ppermute | solution.py:16
  201.5 1.0 fusion.50
  202.5 0.0 copy-start.14
  202.6 0.0 collective-permute-done.3
  202.6 1.0 fusion.51
  203.6 0.0 copy-start
  203.6 0.0 collective-permute-done.2
  203.6 0.3 copy-done.14
  204.0 4.0 %fusion.30 = bf16[1,512,1536]{2,1,0:T(8,128)(2,1)} fusion(bf16[1,512,1536]{2,1,0:T(8,128)(2,1)S(1)} %copy-done.1, f32[512,1536]{1,0:T(8,128)S(1)} %fusion.51, f32[512,1536]{1,0:T(8,128)S(1)} %fusion.50, bf16[512,1536]{1,0:T(8,128)(2,1)S(1)} %copy-done.14, f32[1536]{0:T(1024)S(1)} %copy-done.4, f32[1536]{0:T(1024)S(1)} %copy-done.5, ...), kind=kOutput, calls=%fused_computation.42 | convolution fusion | flops 625213440 | bytes 12623872 | tf_op jit(solution)/shard_map/dot_general | solution.py:85
  207.9 68.3 %all-reduce.3.cloned.1.call-done = bf16[640,1536]{1,0:T(8,128)(2,1)} async-done(((bf16[640,1536]{1,0:T(8,128)(2,1)}), bf16[640,1536]{1,0:T(8,128)(2,1)}) %all-reduce.3.cloned.1.call-update) | async-done | bytes 1966096 | tf_op jit(solution)/shard_map/psum | solution.py:110
  276.2 0.0 copy-done
  276.2 3.4 %subtract_convert_fusion = bf16[640,1536]{1,0:T(8,128)(2,1)} fusion(bf16[640,1536]{1,0:T(8,128)(2,1)} %all-reduce.3.cloned.1.call-done, bf16[640,1536]{1,0:T(8,128)(2,1)S(1)} %copy-done), kind=kLoop, calls=%fused_computation.9 | loop fusion | flops 4915200 | bytes 5898240 | tf_op jit(solution)/shard_map/convert_element_type | solution.py:111
  (15 shorter events, 0.1 us)
Async XLA Ops:
  7.2 11.4 %copy-start.11 = (u32[32]{0:T(128)S(1)}, u32[32]{0:T(128)}, u32[]{:S(2)}) copy-start(u32[32]{0:T(128)} %constant.34) | copy-start | bytes 388
  7.2 5.7 %copy-start.1 = (bf16[1,512,1536]{2,1,0:T(8,128)(2,1)S(1)}, bf16[1,512,1536]{2,1,0:T(8,128)(2,1)}, u32[]{:S(2)}) copy-start(bf16[1,512,1536]{2,1,0:T(8,128)(2,1)} %param.11) | copy-start | bytes 4718596
  7.2 5.7 %copy-start.4 = (f32[1536]{0:T(1024)S(1)}, f32[1536]{0:T(1024)}, u32[]{:S(2)}) copy-start(f32[1536]{0:T(1024)} %param.13) | copy-start | bytes 18436
  7.2 5.7 %copy-start.5 = (f32[1536]{0:T(1024)S(1)}, f32[1536]{0:T(1024)}, u32[]{:S(2)}) copy-start(f32[1536]{0:T(1024)} %param.12) | copy-start | bytes 18436
  7.2 75.1 %all-gather.5.cloned.1.call-start = ((), (), s32[]{:S(2)}) async-start(), calls=%async_computation.1 | async-start | bytes 4423680 | tf_op jit(solution)/shard_map/all_gather | solution.py:41
  7.9 105.0 %all-gather.7.cloned.1.call-start = ((), (), s32[]{:S(2)}) async-start(), calls=%async_computation.2 | async-start | bytes 1474560 | tf_op jit(solution)/shard_map/all_gather | solution.py:42
  8.7 131.6 %all-gather.9.cloned.1.call-start = ((), (), s32[]{:S(2)}) async-start(), calls=%async_computation.5 | async-start | bytes 1769472 | tf_op jit(solution)/shard_map/all_gather | solution.py:73
  12.8 173.9 %reduce-scatter.2.cloned.1.call-start = ((), (), s32[]{:S(2)}) async-start(), calls=%async_computation.3 | async-start | bytes 1769472 | tf_op jit(solution)/shard_map/reduce_scatter | solution.py:101
  14.2 72.9 %collective-permute-start = (bf16[32,1536]{1,0:T(8,128)(2,1)S(1)}, bf16[32,1536]{1,0:T(8,128)(2,1)S(1)}, u32[]{:S(2)}, u32[]{:S(2)}) collective-permute-start(bf16[32,1536]{1,0:T(8,128)(2,1)S(1)} %get-tuple-element.2), channel_id=1, source_target_pairs={{0,1},{1,2},{2,3},{3,4},{4,5},{5,6},{6,7},{8,9},{9,10},{10,11},{11... | collective-permute-start | bytes 294920 | tf_op jit(solution)/shard_map/ppermute | solution.py:16
  16.6 68.6 %collective-permute-start.1 = (bf16[32,1536]{1,0:T(8,128)(2,1)S(1)}, bf16[32,1536]{1,0:T(8,128)(2,1)}, u32[]{:S(2)}, u32[]{:S(2)}) collective-permute-start(bf16[32,1536]{1,0:T(8,128)(2,1)S(1)} %get-tuple-element.3), channel_id=1, source_target_pairs={{1,0},{2,1},{3,2},{4,3},{5,4},{6,5},{7,6},{9,8},{10,9},{11,10},{12... | collective-permute-start | bytes 294920 | tf_op jit(solution)/shard_map/ppermute | solution.py:17
  82.3 2.9 %copy-start.2 = (bf16[1536,3,384]{2,0,1:T(8,128)(2,1)S(1)}, bf16[1536,3,384]{2,0,1:T(8,128)(2,1)}, u32[]{:S(2)}) copy-start(bf16[1536,3,384]{2,0,1:T(8,128)(2,1)} %all-gather.5.cloned.1.call-done) | copy-start | bytes 10616836
  85.1 1.9 copy-start.9
  85.2 1.9 copy-start.10
  115.5 24.8 %copy-start.12 = (bf16[512,1536]{1,0:T(8,128)(2,1)}, bf16[512,1536]{1,0:T(8,128)(2,1)S(1)}, u32[]{:S(2)}) copy-start(bf16[512,1536]{1,0:T(8,128)(2,1)S(1)} %fusion.29) | copy-start | bytes 4718596
  140.3 3.5 %copy-start.8 = (bf16[1,512,512]{2,1,0:T(8,128)(2,1)S(1)}, bf16[1,512,512]{2,1,0:T(8,128)(2,1)}, u32[]{:S(2)}) copy-start(bf16[1,512,512]{2,1,0:T(8,128)(2,1)} %param.19) | copy-start | bytes 1572868
  142.8 1.0 copy-start.13
  143.7 4.4 %copy-start.6 = (bf16[512,1536]{1,0:T(8,128)(2,1)S(1)}, bf16[512,1536]{1,0:T(8,128)(2,1)}, u32[]{:S(2)}) copy-start(bf16[512,1536]{1,0:T(8,128)(2,1)} %all-gather.9.cloned.1.call-done) | copy-start | bytes 4718596
  148.1 128.1 %all-reduce.3.cloned.1.call-start = ((), (), s32[]{:S(2)}) async-start(), calls=%async_computation.4 | async-start | bytes 3932160 | tf_op jit(solution)/shard_map/psum | solution.py:110
  190.4 3.7 %copy-start.7 = (bf16[384,1536]{1,0:T(8,128)(2,1)S(1)}, bf16[384,1536]{1,0:T(8,128)(2,1)}, u32[]{:S(2)}) copy-start(bf16[384,1536]{1,0:T(8,128)(2,1)} %all-gather.7.cloned.1.call-done) | copy-start | bytes 3538948
  194.1 7.4 %copy-start.3 = (bf16[1536,3,384]{2,0,1:T(8,128)(2,1)S(1)}, bf16[1536,3,384]{2,0,1:T(8,128)(2,1)}, u32[]{:S(2)}) copy-start(bf16[1536,3,384]{2,0,1:T(8,128)(2,1)} %all-gather.5.cloned.1.call-done) | copy-start | bytes 10616836
  197.2 6.4 %collective-permute-start.2 = (bf16[32,384]{1,0:T(8,128)(2,1)S(1)}, bf16[32,384]{1,0:T(8,128)(2,1)S(1)}, u32[]{:S(2)}, u32[]{:S(2)}) collective-permute-start(bf16[32,384]{1,0:T(8,128)(2,1)S(1)} %get-tuple-element.4), channel_id=1, source_target_pairs={{1,0},{2,1},{3,2},{4,3},{5,4},{6,5},{7,6},{9,8},{10,9},{11,10},{12... | collective-permute-start | bytes 73736 | tf_op jit(solution)/shard_map/ppermute | solution.py:17
  198.5 4.1 %collective-permute-start.3 = (bf16[32,384]{1,0:T(8,128)(2,1)S(1)}, bf16[32,384]{1,0:T(8,128)(2,1)S(1)}, u32[]{:S(2)}, u32[]{:S(2)}) collective-permute-start(bf16[32,384]{1,0:T(8,128)(2,1)S(1)} %get-tuple-element.5), channel_id=1, source_target_pairs={{0,1},{1,2},{2,3},{3,4},{4,5},{5,6},{6,7},{8,9},{9,10},{10,11},{11... | collective-permute-start | bytes 73736 | tf_op jit(solution)/shard_map/ppermute | solution.py:16
  202.5 1.4 copy-start.14
  203.6 72.6 %copy-start = (bf16[640,1536]{1,0:T(8,128)(2,1)S(1)}, bf16[640,1536]{1,0:T(8,128)(2,1)}, u32[]{:S(2)}) copy-start(bf16[640,1536]{1,0:T(8,128)(2,1)} %param.18) | copy-start | bytes 5898244
Sparse Core Ops, SparseCore 0:
  9.6 72.6 all-gather.4
  83.9 29.0 all-gather.6
  115.4 24.7 all-gather.8
  148.2 38.4 reduce-scatter.1
  194.2 81.9 all-reduce.2
where the time goes:
time: 287 us; the launch traced here: 286 us
  waiting for transfers between devices  198 us (69%)
  matrix products  29 us (10%)
  blocking collectives  17.5 us (6%)
  between operations  15.3 us (5%)
  other arithmetic  12.7 us (4%)
  starting transfers between devices  8.18 us (3%)
  local copies, waits for them, and re-layouts  5.62 us (2%)
    psum x1, waiting for transfers between devices, per_device(): d_head = lax.psum(spread.astype(jnp.bfloat16), 'batch').astype(jnp.float32)  68.3 us
    all_gather x1, waiting for transfers between devices, per_device(): lax.all_gather(dilated_weight, 'batch', axis=0, tiled=True)  44.9 us
    reduce_scatter x1, waiting for transfers between devices, per_device(): lax.psum_scatter(lax.dot_general(delta, embed, (((0,), (0,)), ((), ())),...  34.5 us
    all_gather x1, waiting for transfers between devices, per_device(): lax.all_gather(chosen, 'pos', axis=0, tiled=True)  24.8 us
    all_gather x1, waiting for transfers between devices, per_device(): lax.all_gather(w_point, 'batch', axis=0, tiled=True)  23.9 us
    unnamed x1, blocking collectives  17.5 us
  transfers between devices with their start and end apart: 9, of which 5 were waited for; matrix products, arithmetic and copies ran while one was open for 10% of the time, Pallas kernels for 0%

commit v1 on v0

--- a/solution.py
+++ b/solution.py
@@ -107,7 +107,11 @@
         tiled=True,
     ).astype(jnp.float32)
     spread = jnp.zeros((head.shape[0], owned.shape[1]), jnp.float32).at[slots].add(owned)
-    d_head = lax.psum(spread.astype(jnp.bfloat16), "batch").astype(jnp.float32)
+
+    def lay_samples(packet):
+        return lax.all_gather(packet, "batch").sum(axis=0)
+
+    d_head = lay_samples(spread.astype(jnp.bfloat16)).astype(jnp.float32)
     new_head = (head.astype(jnp.float32) - 0.004 * d_head).astype(jnp.bfloat16)
     return (d_inputs[None], new_head)
 

time: 287 us -> 350 us (1.22)
  waiting for transfers between devices: 198 us -> 259 us
  other arithmetic: 12.7 us -> 18.5 us
    all_gather x0 -> x1, waiting for transfers between devices: none -> 126 us  [lay_samples(): return lax.all_gather(packet, 'batch').sum(axis=0)]
    psum x1 -> x0, waiting for transfers between devices: 68.3 us -> none  [per_device(): d_head = lax.psum(spread.astype(jnp.bfloat16), 'batch').astype(jnp.float32)]
    reduce_sum x0 -> x1, other arithmetic: none -> 5.73 us  [lay_samples(): return lax.all_gather(packet, 'batch').sum(axis=0)]
    reduce_scatter x1, waiting for transfers between devices: 34.5 us -> 38.6 us  [per_device(): lax.psum_scatter(lax.dot_general(delta, embed, (((0,), (0,)), ((), ())),...]
  transfers between devices with their start and end apart: 9 -> 9, of which waited for: 5 -> 5; matrix products, arithmetic and copies ran while one was open for 10% -> 8% of each run, Pallas kernels for 0% -> 0%
where the time goes in v1:
time: 350 us; the launch traced here: 349 us
  waiting for transfers between devices  259 us (74%)
  matrix products  26.4 us (8%)
  other arithmetic  18.5 us (5%)
  blocking collectives  17.4 us (5%)
  between operations  15.4 us (4%)
  starting transfers between devices  8.17 us (2%)
  local copies, waits for them, and re-layouts  4.32 us (1%)
    all_gather x1, waiting for transfers between devices, lay_samples(): return lax.all_gather(packet, 'batch').sum(axis=0)  126 us
    all_gather x1, waiting for transfers between devices, per_device(): lax.all_gather(dilated_weight, 'batch', axis=0, tiled=True)  44.8 us
    reduce_scatter x1, waiting for transfers between devices, per_device(): lax.psum_scatter(lax.dot_general(delta, embed, (((0,), (0,)), ((), ())),...  38.6 us
    all_gather x1, waiting for transfers between devices, per_device(): lax.all_gather(w_point, 'batch', axis=0, tiled=True)  24 us
    all_gather x1, waiting for transfers between devices, per_device(): lax.all_gather(chosen, 'pos', axis=0, tiled=True)  23.6 us
    unnamed x1, blocking collectives  17.4 us
  transfers between devices with their start and end apart: 9, of which 5 were waited for; matrix products, arithmetic and copies ran while one was open for 8% of the time, Pallas kernels for 0%

profile of v1, /device:TPU:0, one launch (start us, length us, event | category | flops | bytes accessed | tf_op | source)
XLA Modules:
  0.0 349.1 jit_solution(9968634959571004362)
XLA Ops:
  7.2 0.0 copy-start.10
  7.2 0.0 copy-start
  7.2 0.0 copy-start.3
  7.2 0.0 copy-start.4
  7.2 0.0 all-gather.7.cloned.1.call-start
  7.3 0.7 all-gather.7.cloned.1.call-update
  7.9 0.0 all-gather.9.cloned.1.call-start
  8.0 0.7 all-gather.9.cloned.1.call-update
  8.7 0.0 all-gather.11.cloned.1.call-start
  8.7 0.7 fusion.71
  9.4 3.4 gather_fusion
  12.8 0.0 all-gather.11.cloned.1.call-update
  12.8 0.0 reduce-scatter.2.cloned.1.call-start
  12.9 0.0 copy-done
  12.9 0.0 copy-done.3
  12.9 0.0 copy-done.4
  12.9 1.3 fusion.12
  14.2 2.4 collective-permute-start
  16.6 1.3 collective-permute-start.1
  18.5 0.0 copy-done.10
  18.5 0.6 dynamic-slice
  19.8 0.2 dynamic-update-slice
  20.0 17.4 %all-reduce = bf16[512]{0:T(512)(128)(2,1)S(1)} all-reduce(bf16[512]{0:T(512)(128)(2,1)S(1)} %dynamic-update-slice), channel_id=1, replica_groups=mesh['batch'=4,'pos'=8] {'pos'}, use_global_device_ids=true, to_apply=%add | all-reduce | flops 512 | bytes 2048
  37.5 44.8 %all-gather.7.cloned.1.call-done = bf16[1536,3,384]{2,0,1:T(8,128)(2,1)} async-done(((bf16[384,3,384]{2,0,1:T(8,128)(2,1)}), bf16[1536,3,384]{2,0,1:T(8,128)(2,1)}) %all-gather.7.cloned.1.call-update) | async-done | bytes 3538960 | tf_op jit(solution)/shard_map/all_gather | solution.py:41
  82.3 2.8 fusion.38
  85.2 0.0 copy-start.9
  85.2 0.0 collective-permute-done.1
  85.2 0.0 copy-done.1
  85.2 1.9 fusion.34
  87.1 0.0 collective-permute-done
  87.1 0.0 copy-done.8
  87.1 0.0 copy-done.9
  87.1 1.9 fusion.44
  89.0 24.0 %all-gather.9.cloned.1.call-done = bf16[384,1536]{1,0:T(8,128)(2,1)} async-done(((bf16[96,1536]{1,0:T(8,128)(2,1)}), bf16[384,1536]{1,0:T(8,128)(2,1)}) %all-gather.9.cloned.1.call-update) | async-done | bytes 1179664 | tf_op jit(solution)/shard_map/all_gather | solution.py:42
  113.0 3.7 %fusion.29 = bf16[512,1536]{1,0:T(8,128)(2,1)} fusion(bf16[384,1536]{1,0:T(8,128)(2,1)} %all-gather.9.cloned.1.call-done, bf16[1,512,1536]{2,1,0:T(8,128)(2,1)S(1)} %copy-done, f32[512,384]{1,0:T(8,128)} %fusion.44), kind=kOutput, calls=%fused_computation.41 | convolution fusion | flops 608108544 | bytes 5111808 | tf_op jit(solution)/shard_map/dot_general | solution.py:66
  116.6 23.6 %all-gather.11.cloned.1.call-done = bf16[512,1536]{1,0:T(8,128)(2,1)} async-done(((bf16[64,1536]{1,0:T(8,128)(2,1)}), bf16[512,1536]{1,0:T(8,128)(2,1)}) %all-gather.11.cloned.1.call-update) | async-done | bytes 1572880 | tf_op jit(solution)/shard_map/all_gather | solution.py:73
  140.3 3.0 fusion.90
  143.3 0.0 copy-done.7
  143.3 0.0 copy-done.11
  143.3 2.8 convolution_convert_fusion
  146.1 0.0 reduce-scatter.2.cloned.1.call-update
  146.2 0.0 all-gather.13.cloned.1.call-start
  146.2 38.6 %reduce-scatter.2.cloned.1.call-done = bf16[64,1536]{1,0:T(8,128)(2,1)} async-done(((bf16[512,1536]{1,0:T(8,128)(2,1)}), bf16[64,1536]{1,0:T(8,128)(2,1)}) %reduce-scatter.2.cloned.1.call-update) | async-done | bytes 196624 | tf_op jit(solution)/shard_map/reduce_scatter | solution.py:101
  184.8 3.7 %scatter_custom_fusion = f32[640,1536]{1,0:T(8,128)} fusion(s32[64]{0:T(128)S(1)} %fusion.71, f32[]{:T(128)} %constant.16.clone.1, bf16[64,1536]{1,0:T(8,128)(2,1)} %reduce-scatter.2.cloned.1.call-done), kind=kCustom, calls=%fused_computation.43 | custom fusion | flops 196608 | bytes 4128772 | tf_op jit(solution)/shard_map/scatter-add | solution.py:109
  188.5 3.7 %convert_element_type.91 = bf16[640,1536]{1,0:T(8,128)(2,1)} convert(f32[640,1536]{1,0:T(8,128)} %scatter_custom_fusion) | non-fusion elementwise | flops 983040 | bytes 5898240 | tf_op jit(solution)/shard_map/convert_element_type | solution.py:114
  192.2 0.0 all-gather.13.cloned.1.call-update
  192.2 0.0 copy-done.5
  192.2 0.0 copy-start.6
  192.3 0.0 copy-start.12
  192.3 3.0 convolution_convert_fusion.1
  195.3 0.0 copy-done.6
  195.3 0.0 copy-done.12
  195.3 0.0 copy-start.2
  195.3 1.3 fusion.45
  196.6 1.3 collective-permute-start.2
  197.9 3.0 collective-permute-start.3
  201.0 1.0 fusion.50
  202.0 0.0 collective-permute-done.3
  202.0 1.0 fusion.51
  203.0 0.0 collective-permute-done.2
  203.0 4.0 %fusion.30 = bf16[1,512,1536]{2,1,0:T(8,128)(2,1)} fusion(bf16[1,512,1536]{2,1,0:T(8,128)(2,1)S(1)} %copy-done, f32[512,1536]{1,0:T(8,128)S(1)} %fusion.51, f32[512,1536]{1,0:T(8,128)S(1)} %fusion.50, bf16[512,1536]{1,0:T(8,128)(2,1)S(1)} %convolution_convert_fusion.1, f32[1536]{0:T(1024)S(1)} %copy-done.3, f32[1536]{0:T(1024)S(1)} %copy-done.4, ...), kind=kOutput, calls=%fused_computation.42 | convolution fusion | flops 625213440 | bytes 12623872 | tf_op jit(solution)/shard_map/dot_general | solution.py:85
  207.0 126.4 %all-gather.13.cloned.1.call-done = bf16[2560,1536]{1,0:T(8,128)(2,1)} async-done(((bf16[640,1536]{1,0:T(8,128)(2,1)}), bf16[2560,1536]{1,0:T(8,128)(2,1)}) %all-gather.13.cloned.1.call-update) | async-done | bytes 7864336 | tf_op jit(solution)/shard_map/all_gather | solution.py:112
  333.4 5.7 %reduce_sum.12 = bf16[640,1536]{1,0:T(8,128)(2,1)S(1)} reduce(bf16[4,640,1536]{2,1,0:T(8,128)(2,1)} %bitcast.94, bf16[]{:T(256)} %constant.5.clone.1), dimensions={0}, to_apply=%region_2.3 | reduce | flops 2949120 | bytes 9830402 | tf_op jit(solution)/shard_map/reduce_sum | solution.py:112
  339.2 3.4 subtract_convert_fusion
  (14 shorter events, 0.1 us)
Async XLA Ops:
  7.2 11.4 %copy-start.10 = (u32[32]{0:T(128)S(1)}, u32[32]{0:T(128)}, u32[]{:S(2)}) copy-start(u32[32]{0:T(128)} %constant.37) | copy-start | bytes 388
  7.2 5.7 %copy-start = (bf16[1,512,1536]{2,1,0:T(8,128)(2,1)S(1)}, bf16[1,512,1536]{2,1,0:T(8,128)(2,1)}, u32[]{:S(2)}) copy-start(bf16[1,512,1536]{2,1,0:T(8,128)(2,1)} %param.11) | copy-start | bytes 4718596
  7.2 5.7 %copy-start.3 = (f32[1536]{0:T(1024)S(1)}, f32[1536]{0:T(1024)}, u32[]{:S(2)}) copy-start(f32[1536]{0:T(1024)} %param.13) | copy-start | bytes 18436
  7.2 5.7 %copy-start.4 = (f32[1536]{0:T(1024)S(1)}, f32[1536]{0:T(1024)}, u32[]{:S(2)}) copy-start(f32[1536]{0:T(1024)} %param.12) | copy-start | bytes 18436
  7.2 75.1 %all-gather.7.cloned.1.call-start = ((), (), s32[]{:S(2)}) async-start(), calls=%async_computation.1 | async-start | bytes 4423680 | tf_op jit(solution)/shard_map/all_gather | solution.py:41
  7.9 105.0 %all-gather.9.cloned.1.call-start = ((), (), s32[]{:S(2)}) async-start(), calls=%async_computation.2 | async-start | bytes 1474560 | tf_op jit(solution)/shard_map/all_gather | solution.py:42
  8.7 131.6 %all-gather.11.cloned.1.call-start = ((), (), s32[]{:S(2)}) async-start(), calls=%async_computation.4 | async-start | bytes 1769472 | tf_op jit(solution)/shard_map/all_gather | solution.py:73
  12.8 172.0 %reduce-scatter.2.cloned.1.call-start = ((), (), s32[]{:S(2)}) async-start(), calls=%async_computation.3 | async-start | bytes 1769472 | tf_op jit(solution)/shard_map/reduce_scatter | solution.py:101
  14.2 72.9 %collective-permute-start = (bf16[32,1536]{1,0:T(8,128)(2,1)S(1)}, bf16[32,1536]{1,0:T(8,128)(2,1)S(1)}, u32[]{:S(2)}, u32[]{:S(2)}) collective-permute-start(bf16[32,1536]{1,0:T(8,128)(2,1)S(1)} %get-tuple-element.2), channel_id=1, source_target_pairs={{0,1},{1,2},{2,3},{3,4},{4,5},{5,6},{6,7},{8,9},{9,10},{10,11},{11... | collective-permute-start | bytes 294920 | tf_op jit(solution)/shard_map/ppermute | solution.py:16
  16.6 68.6 %collective-permute-start.1 = (bf16[32,1536]{1,0:T(8,128)(2,1)S(1)}, bf16[32,1536]{1,0:T(8,128)(2,1)}, u32[]{:S(2)}, u32[]{:S(2)}) collective-permute-start(bf16[32,1536]{1,0:T(8,128)(2,1)S(1)} %get-tuple-element.3), channel_id=1, source_target_pairs={{1,0},{2,1},{3,2},{4,3},{5,4},{6,5},{7,6},{9,8},{10,9},{11,10},{12... | collective-permute-start | bytes 294920 | tf_op jit(solution)/shard_map/ppermute | solution.py:17
  82.3 2.9 copy-start.1
  85.1 1.9 copy-start.8
  85.2 1.9 copy-start.9
  116.6 26.6 %copy-start.7 = (bf16[1,512,512]{2,1,0:T(8,128)(2,1)S(1)}, bf16[1,512,512]{2,1,0:T(8,128)(2,1)}, u32[]{:S(2)}) copy-start(bf16[1,512,512]{2,1,0:T(8,128)(2,1)} %param.19) | copy-start | bytes 1572868
  140.3 3.0 copy-start.11
  143.3 2.8 copy-start.13
  146.2 187.3 %all-gather.13.cloned.1.call-start = ((), (), s32[]{:S(2)}) async-start(), calls=%async_computation.5 | async-start | bytes 9830400 | tf_op jit(solution)/shard_map/all_gather | solution.py:112
  188.5 3.8 %copy-start.5 = (bf16[512,1536]{1,0:T(8,128)(2,1)S(1)}, bf16[512,1536]{1,0:T(8,128)(2,1)}, u32[]{:S(2)}) copy-start(bf16[512,1536]{1,0:T(8,128)(2,1)} %all-gather.11.cloned.1.call-done) | copy-start | bytes 4718596
  192.2 3.1 copy-start.6
  192.3 3.1 copy-start.12
  195.3 5.6 %copy-start.2 = (bf16[1536,3,384]{2,0,1:T(8,128)(2,1)S(1)}, bf16[1536,3,384]{2,0,1:T(8,128)(2,1)}, u32[]{:S(2)}) copy-start(bf16[1536,3,384]{2,0,1:T(8,128)(2,1)} %all-gather.7.cloned.1.call-done) | copy-start | bytes 10616836
  196.6 6.4 %collective-permute-start.2 = (bf16[32,384]{1,0:T(8,128)(2,1)S(1)}, bf16[32,384]{1,0:T(8,128)(2,1)S(1)}, u32[]{:S(2)}, u32[]{:S(2)}) collective-permute-start(bf16[32,384]{1,0:T(8,128)(2,1)S(1)} %get-tuple-element.4), channel_id=1, source_target_pairs={{1,0},{2,1},{3,2},{4,3},{5,4},{6,5},{7,6},{9,8},{10,9},{11,10},{12... | collective-permute-start | bytes 73736 | tf_op jit(solution)/shard_map/ppermute | solution.py:17
  197.9 4.1 %collective-permute-start.3 = (bf16[32,384]{1,0:T(8,128)(2,1)S(1)}, bf16[32,384]{1,0:T(8,128)(2,1)S(1)}, u32[]{:S(2)}, u32[]{:S(2)}) collective-permute-start(bf16[32,384]{1,0:T(8,128)(2,1)S(1)} %get-tuple-element.5), channel_id=1, source_target_pairs={{0,1},{1,2},{2,3},{3,4},{4,5},{5,6},{6,7},{8,9},{9,10},{10,11},{11... | collective-permute-start | bytes 73736 | tf_op jit(solution)/shard_map/ppermute | solution.py:16
Sparse Core Ops, SparseCore 0:
  9.6 72.6 all-gather.6
  83.9 29.0 all-gather.8
  115.4 24.7 all-gather.10
  146.3 38.4 reduce-scatter.1
  192.4 141.0 all-gather.12
